TPU v7x, 256 devices: a whole 4x4x8 slice. The times are simulated.
256 devices in a mesh: ctx: 4 (over z_hi), tp: 8 (over y, core), dec: 8 (over x, z_lo).
Axes of the slice: x: 4, y: 4, z: 8 (z_hi: 4, z_lo: 2; z = z_hi * 2 + z_lo), core: 2. Of those that a mesh axis runs over, the one named last changes fastest.
Arguments:
- cache: bfloat16 [8, 1024, 576], P('dec', 'ctx'), may hold values from -6 to 6
- lengths: int32 [8], P('dec'), may hold values from 1 to 1024
- slot_sequence: int32 [8], replicated, may hold values from 0 to 7, each once
- parents: int32 [8, 64], P('dec'), may hold values from 0 to 62, as said below
- query_nope: bfloat16 [8, 64, 128, 128], P('dec', None, 'tp'), may hold values from -6 to 6
- query_rope: bfloat16 [8, 64, 128, 64], P('dec', None, 'tp'), may hold values from -90 to 90
- new_latent: bfloat16 [8, 64, 576], P('dec'), may hold values from -6 to 6
- key_up: bfloat16 [128, 128, 512], P('tp'), may hold values from -0.5 to 0.5
- value_up: bfloat16 [128, 512, 128], P('tp'), may hold values from -0.25 to 0.25
- out_proj: bfloat16 [16384, 7168], P('tp', ('ctx', 'dec')), may hold values from -0.046875 to 0.046875
Outputs:
- attended: bfloat16 [8, 64, 7168], P(None, 'tp', ('ctx', 'dec'))
Inputs may be any that keep to these rules, and one draw needn't show every extreme that they name: `slot_sequence`: every sequence is held by exactly one slot. parents[s, 0] = 0 and parents[s, i] < i for every i >= 1.
All inputs are finite; a program needn't handle non-finite values.
Results may differ from a plain program's by a relative error of at most 0.024.
Values may be sent and summed in bfloat16 or wider, within the bound.
A program may use at most 64 MiB of HBM per device.

v0:
```python
import math
import jax
import jax.numpy as jnp
from jax import lax
from jax.sharding import PartitionSpec as P


def joined_along(blocks, dim):
    shape = list(blocks.shape[1:])
    shape[dim] *= blocks.shape[0]
    return jnp.moveaxis(blocks, 0, dim).reshape(shape)


def sent_to_all(value, axis):
    copies = jnp.broadcast_to(value, (lax.axis_size(axis), *value.shape))
    return lax.all_to_all(copies, axis, split_axis=0, concat_axis=0, tiled=True)


def collect(value, axis, dim):
    return joined_along(sent_to_all(value, axis), dim)


def sent_together(arrays, axis, dim, along):
    columns = [a.reshape(*a.shape[:along], -1) for a in arrays]
    both = jnp.concatenate(columns, axis=along)
    whole, at, done = (collect(both, axis, dim), 0, [])
    for a, column in zip(arrays, columns):
        piece = whole[..., at : at + column.shape[along]]
        done.append(piece.reshape(*piece.shape[:along], *a.shape[along:]))
        at += column.shape[along]
    return tuple(done)


def for_sending(value):

    def short(part):
        return part.astype(jnp.bfloat16) if part.dtype == jnp.float32 else part

    return jax.tree.map(short, value)


def in_blocks(value, dim, size):
    before, after = (value.shape[:dim], value.shape[dim + 1 :])
    return jnp.moveaxis(value.reshape(*before, size, -1, *after), dim, 0)


def sent_and_summed(value, axis, dim):
    size = lax.axis_size(axis)
    blocks = lax.all_to_all(in_blocks(value, dim, size), axis, 0, 0, tiled=True)
    return jnp.sum(blocks.astype(jnp.float32), axis=0)


def ancestors(parents):
    node_count = parents.shape[-1]
    node_ids = jnp.arange(node_count, dtype=jnp.int32)
    parent_link = (parents[..., :, None] == node_ids).astype(jnp.float32)
    closure = jnp.maximum(parent_link, jnp.eye(node_count, dtype=jnp.float32))
    for _ in range(node_count.bit_length()):
        closure = jnp.minimum(
            jnp.einsum("sij,sjk->sik", closure, closure, precision=lax.Precision.HIGHEST), 1.0
        )
    return closure


def partial_softmax(queries, key_rows, live_mask, latent, score_scale):
    scores = (
        jnp.einsum("snhc,spc->snhp", queries, key_rows, preferred_element_type=jnp.float32)
        * score_scale
    )
    alive = live_mask > 0
    scores = jnp.where(alive, scores, -1e30)
    row_peak = jnp.max(scores, axis=-1)
    expo = jnp.where(alive, jnp.exp(scores - row_peak[..., None]), 0.0)
    row_total = jnp.sum(expo, axis=-1)
    weighted = jnp.einsum(
        "snhp,spc->snhc",
        expo.astype(jnp.bfloat16),
        key_rows[..., :latent],
        preferred_element_type=jnp.float32,
    )
    return (row_peak, row_total, weighted)


def join_parts(first_part, second_part):
    new_peak = jnp.maximum(first_part[0], second_part[0])
    first_factor = jnp.exp(first_part[0] - new_peak)
    second_factor = jnp.exp(second_part[0] - new_peak)
    row_total = first_part[1] * first_factor + second_part[1] * second_factor
    weighted = first_part[2] * first_factor[..., None] + second_part[2] * second_factor[..., None]
    return (new_peak, row_total, weighted)


def pick_rows(select, pieces):
    flat_rows = pieces.reshape(pieces.shape[0], -1)
    chosen = jnp.dot(select, flat_rows, preferred_element_type=jnp.float32)
    return chosen.reshape((select.shape[0],) + pieces.shape[1:]).astype(pieces.dtype)


def to_values(part, value_weight):
    projected = jnp.einsum("snhc,hcv->snhv", part[2], value_weight, precision=lax.Precision.HIGHEST)
    return (part[0], part[1], projected)


def on_device(
    cache,
    lengths,
    slot_sequence,
    parents,
    query_nope,
    query_rope,
    new_latent,
    key_up,
    value_up,
    out_proj,
):
    seq_dev = cache.shape[0]
    ctx_len = cache.shape[1]
    latent = value_up.shape[1]
    node_count = parents.shape[1]
    ctx_count = lax.axis_size("ctx")
    dec_count = lax.axis_size("dec")
    ctx_at = lax.axis_index("ctx")
    dec_at = lax.axis_index("dec")
    score_scale = 1.0 / math.sqrt(key_up.shape[1] + cache.shape[2] - latent)
    positions = ctx_at * ctx_len + jnp.arange(ctx_len, dtype=jnp.int32)
    valid = (positions[None, :] < lengths[:, None]).astype(jnp.bfloat16)
    tree_local = ancestors(parents).astype(jnp.bfloat16)
    value_weight = value_up.astype(jnp.float32)
    wanted = lax.dynamic_slice_in_dim(slot_sequence, dec_at * seq_dev, seq_dev)
    pieces = sent_together((cache, valid), "dec", 0, 2)
    piece_count = pieces[0].shape[0]
    sources = jnp.arange(piece_count, dtype=jnp.int32)
    select = (wanted[:, None] == sources[None, :]).astype(jnp.bfloat16)
    key_rows = pick_rows(select, pieces[0])
    live_rows = pick_rows(select, pieces[1])
    nope_rows, rope_rows, tree_keys, tree_mask = (query_nope, query_rope, new_latent, tree_local)
    absorbed = jnp.einsum(
        "snhd,hdc->snhc", nope_rows, key_up, preferred_element_type=jnp.float32
    ).astype(jnp.bfloat16)
    queries = jnp.concatenate([absorbed, rope_rows], axis=-1)
    cache_part = partial_softmax(
        queries, key_rows, live_rows[:, None, None, :], latent, score_scale
    )
    cache_part = to_values(cache_part, value_weight)
    node_block = node_count // ctx_count
    first_node = ctx_at * node_block
    stacked = tuple((member[None] for member in cache_part))
    spread = jax.tree.map(
        lambda part, own: part.astype(own.dtype),
        lax.all_to_all(for_sending(stacked), "ctx", split_axis=2, concat_axis=0, tiled=True),
        stacked,
    )
    peak_all = jnp.max(spread[0], axis=0)
    factors = jnp.exp(spread[0] - peak_all[None])
    merged = (
        peak_all,
        jnp.sum(spread[1] * factors, axis=0),
        jnp.sum(spread[2] * factors[..., None], axis=0),
    )
    block_queries = lax.dynamic_slice_in_dim(queries, first_node, node_block, 1)
    block_tree = lax.dynamic_slice_in_dim(tree_mask, first_node, node_block, 1)
    tree_part = partial_softmax(
        block_queries, tree_keys, block_tree[:, :, None, :], latent, score_scale
    )
    tree_part = to_values(tree_part, value_weight)
    final = join_parts(merged, tree_part)
    head_values = (final[2] / final[1][..., None]).astype(jnp.bfloat16)
    head_values = head_values.reshape(seq_dev, node_block, -1)
    projected = jnp.einsum(
        "ksnv,vd->ksnd",
        lax.all_gather(head_values[None], ("ctx", "dec"), axis=0, tiled=True),
        out_proj,
        preferred_element_type=jnp.float32,
    )
    column_count = out_proj.shape[1]
    projected = projected.reshape(ctx_count, dec_count, seq_dev, node_block, column_count)
    projected = projected.transpose(1, 2, 0, 3, 4).reshape(
        dec_count * seq_dev, node_count, column_count
    )
    return sent_and_summed(projected.astype(jnp.bfloat16), "tp", 1).astype(jnp.bfloat16)


def solution(mesh):
    return jax.shard_map(
        on_device,
        mesh=mesh,
        in_specs=(
            P("dec", "ctx", None),
            P("dec"),
            P(),
            P("dec", None),
            P("dec", None, "tp", None),
            P("dec", None, "tp", None),
            P("dec", None, None),
            P("tp", None, None),
            P("tp", None, None),
            P("tp", ("ctx", "dec")),
        ),
        out_specs=P(None, "tp", ("ctx", "dec")),
        check_vma=False,
    )
```

profile of v0, /device:TPU:1, one launch (start us, length us, event | category | flops | bytes accessed | tf_op | source)
XLA Modules:
  0.0 289.7 jit_solution(6729289213615725984)
XLA Ops:
  7.4 1.0 maximum_bitcast_fusion
  8.3 1.6 broadcast_in_dim.58
  9.9 6.3 %all-to-all-start = ((bf16[8,1,256,577]{2,3,1,0:T(8,128)(2,1)}), bf16[8,1,256,577]{2,3,1,0:T(8,128)(2,1)}, u32[]{:S(2)}, u32[]{:S(2)}) async-start(bf16[8,1,256,577]{2,3,1,0:T(8,128)(2,1)} %broadcast_in_dim.58), calls=%async_computation | async-start | bytes 4784128 | tf_op jit(solution)/shard_map/all_to_all | solution.py:16
  16.3 0.1 fusion.37
  16.5 0.2 convolution_minimum_fusion.5
  16.7 0.2 convolution_minimum_fusion.4
  16.8 0.2 convolution_minimum_fusion.3
  17.0 0.2 convolution_minimum_fusion.2
  17.2 0.2 convolution_minimum_fusion.1
  17.3 0.2 convolution_minimum_fusion
  17.5 0.2 fusion.51
  17.7 1.4 fusion.2
  19.2 0.9 fusion.49
  20.1 0.7 copy.129
  20.8 1.7 fusion.30
  22.5 1.4 copy.136
  23.9 1.3 dynamic_slice.7
  25.1 1.2 bitcast_convert_fusion
  26.3 1.2 fusion.4
  27.5 0.2 fusion.33
  27.7 17.5 %all-to-all-done = bf16[8,1,256,577]{2,3,1,0:T(8,128)(2,1)} async-done(((bf16[8,1,256,577]{2,3,1,0:T(8,128)(2,1)}), bf16[8,1,256,577]{2,3,1,0:T(8,128)(2,1)}, u32[]{:S(2)}, u32[]{:S(2)}) %all-to-all-start) | async-done | bytes 2363424 | tf_op jit(solution)/shard_map/all_to_all | solution.py:16
  45.2 2.2 copy.165
  47.4 0.7 fusion.42
  48.1 1.6 slice.17
  49.7 4.8 %copy.118 = bf16[8,256,576]{2,1,0:T(8,128)(2,1)} copy(bf16[8,256,576]{1,0,2:T(8,128)(2,1)} %slice.17) | data formatting | bytes 4718592 | tf_op jit(solution)/shard_map/slice | solution.py:28
  54.5 5.8 %reshape.529 = bf16[1179648]{0:T(1024)(128)(2,1)} reshape(bf16[8,256,576]{2,1,0:T(8,128)(2,1)} %copy.118) | data formatting | bytes 4718592
  60.4 4.1 %reshape.511 = bf16[8,147456]{1,0:T(8,128)(2,1)} reshape(bf16[1179648]{0:T(1024)(128)(2,1)} %reshape.529) | data formatting | bytes 4718592 | tf_op jit(solution)/shard_map/reshape | solution.py:94
  64.4 4.2 %reshape.531 = bf16[1179648]{0:T(1024)(128)(2,1)} reshape(bf16[8,147456]{1,0:T(8,128)(2,1)} %reshape.511) | data formatting | bytes 4718592
  68.6 5.5 %reshape.532 = bf16[8,256,576]{2,1,0:T(8,128)(2,1)} reshape(bf16[1179648]{0:T(1024)(128)(2,1)} %reshape.531) | data formatting | bytes 4718592
  74.1 2.5 multiply_reduce_fusion
  76.6 2.0 fusion.50
  78.7 1.6 fusion.19
  80.3 0.1 copy.124
  80.4 0.6 broadcast.166
  81.0 0.8 reduce.17
  81.8 0.7 reshape.533
  82.4 7.7 %all-to-all-start.2 = ((bf16[4,2,128]{2,1,0:T(2,128)(2,1)}), bf16[4,2,128]{2,1,0:T(2,128)(2,1)S(1)}, u32[]{:S(2)}, u32[]{:S(2)}) async-start(bf16[4,2,128]{2,1,0:T(2,128)(2,1)} %reshape.533), calls=%async_computation.2 | async-start | bytes 4096 | tf_op jit(solution)/shard_map/all_to_all | solution.py:150
  90.1 0.4 fusion.22
  90.5 1.1 copy-done.1
  91.7 1.3 fusion.12
  93.0 0.1 copy.132
  93.0 0.1 copy.133
  93.2 0.8 reduce.18
  93.9 0.7 reshape.535
  94.6 0.9 copy.122
  95.5 1.1 all-to-all-done.2
  96.6 5.5 %all-to-all-start.3 = ((bf16[4,2,128]{2,1,0:T(2,128)(2,1)}), bf16[4,2,128]{2,1,0:T(2,128)(2,1)S(1)}, u32[]{:S(2)}, u32[]{:S(2)}) async-start(bf16[4,2,128]{2,1,0:T(2,128)(2,1)} %reshape.535), calls=%async_computation.3 | async-start | bytes 4096 | tf_op jit(solution)/shard_map/all_to_all | solution.py:150
  102.1 0.1 reshape.534
  102.3 0.1 copy.125
  102.3 0.1 all_to_all.15
  102.5 6.0 %all-to-all-done.3 = bf16[4,2,128]{2,1,0:T(2,128)(2,1)S(1)} async-done(((bf16[4,2,128]{2,1,0:T(2,128)(2,1)}), bf16[4,2,128]{2,1,0:T(2,128)(2,1)S(1)}, u32[]{:S(2)}, u32[]{:S(2)}) %all-to-all-start.3) | async-done | bytes 2080 | tf_op jit(solution)/shard_map/all_to_all | solution.py:150
  108.5 3.4 %all-to-all-start.1 = ((bf16[1,1,64,16,128]{4,3,1,0,2:T(8,128)(2,1)}), bf16[1,1,64,16,128]{4,3,1,0,2:T(8,128)(2,1)S(1)}, u32[]{:S(2)}, u32[]{:S(2)}) async-start(bf16[1,1,64,16,128]{4,3,1,0,2:T(8,128)(2,1)} %copy.122), calls=%async_computation.1 | async-start | bytes 524288 | tf_op jit(solution)/shard_map/all_to_all | solution.py:150
  111.9 0.1 reshape.536
  112.1 0.1 copy.134
  112.2 0.1 copy.126
  112.3 0.1 copy.135
  112.4 7.5 %all-to-all-done.1 = bf16[1,1,64,16,128]{4,3,1,0,2:T(8,128)(2,1)S(1)} async-done(((bf16[1,1,64,16,128]{4,3,1,0,2:T(8,128)(2,1)}), bf16[1,1,64,16,128]{4,3,1,0,2:T(8,128)(2,1)S(1)}, u32[]{:S(2)}, u32[]{:S(2)}) %all-to-all-start.1) | async-done | bytes 262176 | tf_op jit(solution)/shard_map/all_to_all | solution.py:150
  119.9 0.2 fusion.21
  120.1 2.5 fusion.17
  122.7 0.7 broadcast_in_dim_reshape.3
  123.4 126.0 %all-gather.2.cloned.1.call-done = bf16[32,1,16,2048]{3,2,1,0:T(8,128)(2,1)} async-done(((bf16[1,1,16,2048]{3,2,1,0:T(8,128)(2,1)}), bf16[32,1,16,2048]{3,2,1,0:T(8,128)(2,1)}) %all-gather.2.cloned.1.call-update) | async-done | bytes 2097168 | tf_op jit(solution)/shard_map/all_gather | solution.py:171
  249.4 2.5 fusion.9
  252.0 30.2 %all_to_all.40 = bf16[8,8,8,224]{3,2,1,0:T(8,128)(2,1)S(1)} all-to-all(bf16[8,8,8,224]{3,2,1,0:T(8,128)(2,1)S(1)} %copy.139), channel_id=1, replica_groups=mesh['ctx'=4,'tp'=8,'dec'=8] {'tp'}, dimensions={0} | all-to-all | bytes 458752 | tf_op jit(solution)/shard_map/all_to_all | solution.py:49
  282.2 0.7 reduce_sum.55
  (39 shorter events, 0.5 us)
Async XLA Ops:
  6.5 11.2 %copy-start = (bf16[16,128,512]{2,1,0:T(8,128)(2,1)S(1)}, bf16[16,128,512]{2,1,0:T(8,128)(2,1)}, u32[]{:S(2)}) copy-start(bf16[16,128,512]{2,1,0:T(8,128)(2,1)} %param.17) | copy-start | bytes 6291460
  9.9 6.3 %copy-start.3 = (bf16[1,64,16,64]{3,2,1,0:T(8,128)(2,1)S(1)}, bf16[1,64,16,64]{3,2,1,0:T(8,128)(2,1)}, u32[]{:S(2)}) copy-start(bf16[1,64,16,64]{3,2,1,0:T(8,128)(2,1)} %param.15) | copy-start | bytes 393220
  9.9 6.4 %copy-start.9 = (s32[1,64]{1,0:T(1,128)S(1)}, s32[1,64]{1,0:T(1,128)}, u32[]{:S(2)}) copy-start(s32[1,64]{1,0:T(1,128)} %param.13) | copy-start | bytes 772
  9.9 35.3 %all-to-all-start = ((bf16[8,1,256,577]{2,3,1,0:T(8,128)(2,1)}), bf16[8,1,256,577]{2,3,1,0:T(8,128)(2,1)}, u32[]{:S(2)}, u32[]{:S(2)}) async-start(bf16[8,1,256,577]{2,3,1,0:T(8,128)(2,1)} %broadcast_in_dim.58), calls=%async_computation | async-start | bytes 4784128 | tf_op jit(solution)/shard_map/all_to_all | solution.py:16
  17.7 1.5 copy-start.8
  17.7 1.5 copy-start.4
  20.1 0.7 copy-start.7
  68.6 5.5 %copy-start.10 = (f32[8]{0:T(128)S(1)}, f32[8]{0:T(128)}, u32[]{:S(2)}) copy-start(f32[8]{0:T(128)} %bitcast_convert_fusion) | copy-start | bytes 100
  74.1 2.5 copy-start.2
  82.4 14.2 %all-to-all-start.2 = ((bf16[4,2,128]{2,1,0:T(2,128)(2,1)}), bf16[4,2,128]{2,1,0:T(2,128)(2,1)S(1)}, u32[]{:S(2)}, u32[]{:S(2)}) async-start(bf16[4,2,128]{2,1,0:T(2,128)(2,1)} %reshape.533), calls=%async_computation.2 | async-start | bytes 4096 | tf_op jit(solution)/shard_map/all_to_all | solution.py:150
  90.1 1.6 copy-start.1
  91.7 20.7 %copy-start.5 = (f32[16,16]{0,1:T(8,128)S(1)}, f32[16,16]{0,1:T(8,128)}, u32[]{:S(2)}) copy-start(f32[16,16]{0,1:T(8,128)} %copy.129) | copy-start | bytes 3076
  91.7 20.7 %copy-start.6 = (f32[16,16]{0,1:T(8,128)S(1)}, f32[16,16]{0,1:T(8,128)}, u32[]{:S(2)}) copy-start(f32[16,16]{0,1:T(8,128)} %copy.136) | copy-start | bytes 3076
  96.6 11.9 %all-to-all-start.3 = ((bf16[4,2,128]{2,1,0:T(2,128)(2,1)}), bf16[4,2,128]{2,1,0:T(2,128)(2,1)S(1)}, u32[]{:S(2)}, u32[]{:S(2)}) async-start(bf16[4,2,128]{2,1,0:T(2,128)(2,1)} %reshape.535), calls=%async_computation.3 | async-start | bytes 4096 | tf_op jit(solution)/shard_map/all_to_all | solution.py:150
  108.5 11.4 %all-to-all-start.1 = ((bf16[1,1,64,16,128]{4,3,1,0,2:T(8,128)(2,1)}), bf16[1,1,64,16,128]{4,3,1,0,2:T(8,128)(2,1)S(1)}, u32[]{:S(2)}, u32[]{:S(2)}) async-start(bf16[1,1,64,16,128]{4,3,1,0,2:T(8,128)(2,1)} %copy.122), calls=%async_computation.1 | async-start | bytes 524288 | tf_op jit(solution)/shard_map/all_to_all | solution.py:150
  111.9 137.5 %all-gather.2.cloned.1.call-start = ((), (), s32[]{:S(2)}) async-start(), calls=%async_computation.5 | async-start | bytes 2162688 | tf_op jit(solution)/shard_map/all_gather | solution.py:171
Sparse Core Ops, SparseCore 0:
  123.5 125.8 all-gather.1
where the time goes:
time: 291 us; the launch traced here: 290 us
  waiting for transfers between devices  158 us (54%)
  local copies, waits for them, and re-layouts  38.7 us (13%)
  blocking collectives  30.2 us (10%)
  starting transfers between devices  23 us (8%)
  between operations  14.5 us (5%)
  matrix products  13.2 us (5%)
  other arithmetic  12 us (4%)
    all_gather x1, waiting for transfers between devices, on_device(): lax.all_gather(head_values[None], ('ctx', 'dec'), axis=0, tiled=True)  126 us
    all_to_all x1, blocking collectives, sent_and_summed(): blocks = lax.all_to_all(in_blocks(value, dim, size), axis, 0, 0, tiled=True)  30.2 us
    unnamed x31, local copies, waits for them, and re-layouts  18.9 us
    all_to_all x1, waiting for transfers between devices, sent_to_all(): return lax.all_to_all(copies, axis, split_axis=0, concat_axis=0, tiled=True)  17.5 us
    all_to_all x3, starting transfers between devices, on_device(): lax.all_to_all(for_sending(stacked), 'ctx', split_axis=2, concat_axis=0,...  16.6 us
    all_to_all x3, waiting for transfers between devices, on_device(): lax.all_to_all(for_sending(stacked), 'ctx', split_axis=2, concat_axis=0,...  14.7 us
    slice x2, local copies, waits for them, and re-layouts, sent_together(): piece = whole[..., at:at + column.shape[along]]  6.41 us
    all_to_all x1, starting transfers between devices, sent_to_all(): return lax.all_to_all(copies, axis, split_axis=0, concat_axis=0, tiled=True)  6.33 us
  transfers between devices with their start and end apart: 5, of which 5 were waited for; matrix products, arithmetic and copies ran while one was open for 6% of the time, Pallas kernels for 0%

commit v1 on v0

--- a/solution.py
+++ b/solution.py
@@ -168,7 +168,12 @@
     head_values = head_values.reshape(seq_dev, node_block, -1)
     projected = jnp.einsum(
         "ksnv,vd->ksnd",
-        lax.all_gather(head_values[None], ("ctx", "dec"), axis=0, tiled=True),
+        jnp.concatenate(
+            lax.all_to_all(
+                jnp.stack([head_values[None]] * lax.axis_size(("ctx", "dec"))), ("ctx", "dec"), 0, 0
+            ),
+            axis=0,
+        ),
         out_proj,
         preferred_element_type=jnp.float32,
     )

time: 291 us -> 186 us (0.64)
  waiting for transfers between devices: 158 us -> 32.2 us
  blocking collectives: 30.2 us -> 66.7 us
  between operations: 14.5 us -> 1.15 us
    all_gather x1 -> x0, waiting for transfers between devices: 126 us -> none  [on_device(): lax.all_gather(head_values[None], ('ctx', 'dec'), axis=0, tiled=True)]
    all_to_all x0 -> x1, blocking collectives: none -> 50.4 us  [on_device(): lax.all_to_all(jnp.stack([head_values[None]] * lax.axis_size(('ctx', 'dec...]
    all_to_all x1, blocking collectives: 30.2 us -> 16.3 us  [sent_and_summed(): blocks = lax.all_to_all(in_blocks(value, dim, size), axis, 0, 0, tiled=True)]
    unnamed x31 -> x34, local copies, waits for them, and re-layouts: 18.9 us -> 18.9 us
  transfers between devices with their start and end apart: 5 -> 4, of which waited for: 5 -> 4; matrix products, arithmetic and copies ran while one was open for 6% -> 9% of each run, Pallas kernels for 0% -> 0%
where the time goes in v1:
time: 186 us; the launch traced here: 185 us
  blocking collectives  66.7 us (36%)
  local copies, waits for them, and re-layouts  38.3 us (21%)
  waiting for transfers between devices  32.2 us (17%)
  starting transfers between devices  22.9 us (12%)
  other arithmetic  12 us (6%)
  matrix products  11.4 us (6%)
    all_to_all x1, blocking collectives, on_device(): lax.all_to_all(jnp.stack([head_values[None]] * lax.axis_size(('ctx', 'dec...  50.4 us
    unnamed x34, local copies, waits for them, and re-layouts  18.9 us
    all_to_all x1, waiting for transfers between devices, sent_to_all(): return lax.all_to_all(copies, axis, split_axis=0, concat_axis=0, tiled=True)  17.5 us
    all_to_all x3, starting transfers between devices, on_device(): lax.all_to_all(for_sending(stacked), 'ctx', split_axis=2, concat_axis=0,...  16.6 us
    all_to_all x1, blocking collectives, sent_and_summed(): blocks = lax.all_to_all(in_blocks(value, dim, size), axis, 0, 0, tiled=True)  16.3 us
    all_to_all x3, waiting for transfers between devices, on_device(): lax.all_to_all(for_sending(stacked), 'ctx', split_axis=2, concat_axis=0,...  14.7 us
    slice x2, local copies, waits for them, and re-layouts, sent_together(): piece = whole[..., at:at + column.shape[along]]  6.41 us
    all_to_all x1, starting transfers between devices, sent_to_all(): return lax.all_to_all(copies, axis, split_axis=0, concat_axis=0, tiled=True)  6.33 us
  transfers between devices with their start and end apart: 4, of which 4 were waited for; matrix products, arithmetic and copies ran while one was open for 9% of the time, Pallas kernels for 0%

profile of v1, /device:TPU:1, one launch (start us, length us, event | category | flops | bytes accessed | tf_op | source)
XLA Modules:
  0.0 184.7 jit_solution(476925457785280670)
XLA Ops:
  0.8 1.0 maximum_bitcast_fusion
  1.8 1.6 broadcast_in_dim.58
  3.4 6.3 %all-to-all-start = ((bf16[8,1,256,577]{2,3,1,0:T(8,128)(2,1)}), bf16[8,1,256,577]{2,3,1,0:T(8,128)(2,1)}, u32[]{:S(2)}, u32[]{:S(2)}) async-start(bf16[8,1,256,577]{2,3,1,0:T(8,128)(2,1)} %broadcast_in_dim.58), calls=%async_computation | async-start | bytes 4784128 | tf_op jit(solution)/shard_map/all_to_all | solution.py:16
  9.8 0.1 fusion.30
  10.0 0.2 convolution_minimum_fusion.5
  10.1 0.2 convolution_minimum_fusion.4
  10.3 0.2 convolution_minimum_fusion.3
  10.5 0.2 convolution_minimum_fusion.2
  10.6 0.2 convolution_minimum_fusion.1
  10.8 0.2 convolution_minimum_fusion
  11.0 0.2 fusion.44
  11.2 1.4 fusion
  12.7 0.9 fusion.42
  13.6 0.7 copy.129
  14.2 1.7 fusion.23
  16.0 1.4 copy.136
  17.3 1.3 dynamic_slice.7
  18.6 1.2 bitcast_convert_fusion
  19.8 1.2 fusion.2
  21.0 0.2 fusion.26
  21.2 17.5 %all-to-all-done = bf16[8,1,256,577]{2,3,1,0:T(8,128)(2,1)} async-done(((bf16[8,1,256,577]{2,3,1,0:T(8,128)(2,1)}), bf16[8,1,256,577]{2,3,1,0:T(8,128)(2,1)}, u32[]{:S(2)}, u32[]{:S(2)}) %all-to-all-start) | async-done | bytes 2363424 | tf_op jit(solution)/shard_map/all_to_all | solution.py:16
  38.7 2.2 %copy.167 = bf16[8,1,256,577]{2,0,3,1:T(8,128)(2,1)S(1)} copy(bf16[8,1,256,577]{2,3,1,0:T(8,128)(2,1)} %all-to-all-done) | data formatting | bytes 4726784 | tf_op jit(solution)/shard_map/all_to_all | solution.py:16
  40.8 0.7 fusion.35
  41.6 1.6 slice.17
  43.2 4.8 %copy.118 = bf16[8,256,576]{2,1,0:T(8,128)(2,1)} copy(bf16[8,256,576]{1,0,2:T(8,128)(2,1)} %slice.17) | data formatting | bytes 4718592 | tf_op jit(solution)/shard_map/slice | solution.py:28
  48.0 5.8 %reshape.535 = bf16[1179648]{0:T(1024)(128)(2,1)} reshape(bf16[8,256,576]{2,1,0:T(8,128)(2,1)} %copy.118) | data formatting | bytes 4718592
  53.8 4.1 %reshape.517 = bf16[8,147456]{1,0:T(8,128)(2,1)} reshape(bf16[1179648]{0:T(1024)(128)(2,1)} %reshape.535) | data formatting | bytes 4718592 | tf_op jit(solution)/shard_map/reshape | solution.py:94
  57.9 4.2 %reshape.537 = bf16[1179648]{0:T(1024)(128)(2,1)} reshape(bf16[8,147456]{1,0:T(8,128)(2,1)} %reshape.517) | data formatting | bytes 4718592
  62.1 5.5 %reshape.538 = bf16[8,256,576]{2,1,0:T(8,128)(2,1)} reshape(bf16[1179648]{0:T(1024)(128)(2,1)} %reshape.537) | data formatting | bytes 4718592
  67.6 2.5 %multiply_reduce_fusion = bf16[256,576]{1,0:T(8,128)(2,1)S(1)} fusion(f32[8]{0:T(128)S(1)} %copy-done.10, bf16[8,256,576]{2,1,0:T(8,128)(2,1)} %reshape.538), kind=kLoop, calls=%fused_computation | loop fusion | flops 3391488 | bytes 2654240 | tf_op jit(solution)/shard_map/dot_general | solution.py:95
  70.1 2.0 %fusion.43 = (f32[64,16]{1,0:T(8,128)S(1)}, f32[64,16,256]{2,1,0:T(8,128)}) fusion(bf16[256,576]{1,0:T(8,128)(2,1)S(1)} %multiply_reduce_fusion, bf16[64,16,576]{2,0,1:T(8,128)(2,1)S(1)} %copy-done.2, pred[256]{0:T(512)(128)(4,1)S(1)} %convert_compare_fusion), kind=kOutput, calls=%fused_computation.80 | convolution fusion | flops 302775296 | bytes 2527488 | tf_op jit(solution)/shard_map/snhc,spc->snhp/dot_general | solution.py:67
  72.1 1.6 fusion.12
  73.7 0.1 copy.124
  73.8 0.6 broadcast.168
  74.4 0.8 reduce.17
  75.2 0.7 reshape.539
  75.9 7.7 %all-to-all-start.2 = ((bf16[4,2,128]{2,1,0:T(2,128)(2,1)}), bf16[4,2,128]{2,1,0:T(2,128)(2,1)S(1)}, u32[]{:S(2)}, u32[]{:S(2)}) async-start(bf16[4,2,128]{2,1,0:T(2,128)(2,1)} %reshape.539), calls=%async_computation.2 | async-start | bytes 4096 | tf_op jit(solution)/shard_map/all_to_all | solution.py:150
  83.6 0.4 fusion.15
  84.0 1.1 copy-done.1
  85.1 1.3 fusion.5
  86.4 0.1 copy.132
  86.5 0.1 copy.133
  86.6 0.8 reduce.18
  87.4 0.7 reshape.541
  88.1 0.9 copy.122
  88.9 1.1 all-to-all-done.2
  90.1 5.5 %all-to-all-start.3 = ((bf16[4,2,128]{2,1,0:T(2,128)(2,1)}), bf16[4,2,128]{2,1,0:T(2,128)(2,1)S(1)}, u32[]{:S(2)}, u32[]{:S(2)}) async-start(bf16[4,2,128]{2,1,0:T(2,128)(2,1)} %reshape.541), calls=%async_computation.3 | async-start | bytes 4096 | tf_op jit(solution)/shard_map/all_to_all | solution.py:150
  95.6 0.1 reshape.540
  95.7 0.1 copy.125
  95.8 0.1 all_to_all.17
  95.9 6.0 %all-to-all-done.3 = bf16[4,2,128]{2,1,0:T(2,128)(2,1)S(1)} async-done(((bf16[4,2,128]{2,1,0:T(2,128)(2,1)}), bf16[4,2,128]{2,1,0:T(2,128)(2,1)S(1)}, u32[]{:S(2)}, u32[]{:S(2)}) %all-to-all-start.3) | async-done | bytes 2080 | tf_op jit(solution)/shard_map/all_to_all | solution.py:150
  102.0 3.4 %all-to-all-start.1 = ((bf16[1,1,64,16,128]{4,3,1,0,2:T(8,128)(2,1)}), bf16[1,1,64,16,128]{4,3,1,0,2:T(8,128)(2,1)S(1)}, u32[]{:S(2)}, u32[]{:S(2)}) async-start(bf16[1,1,64,16,128]{4,3,1,0,2:T(8,128)(2,1)} %copy.122), calls=%async_computation.1 | async-start | bytes 524288 | tf_op jit(solution)/shard_map/all_to_all | solution.py:150
  105.4 0.1 reshape.542
  105.5 0.1 copy.134
  105.6 0.1 copy.126
  105.7 0.1 copy.135
  105.8 7.6 %all-to-all-done.1 = bf16[1,1,64,16,128]{4,3,1,0,2:T(8,128)(2,1)S(1)} async-done(((bf16[1,1,64,16,128]{4,3,1,0,2:T(8,128)(2,1)}), bf16[1,1,64,16,128]{4,3,1,0,2:T(8,128)(2,1)S(1)}, u32[]{:S(2)}, u32[]{:S(2)}) %all-to-all-start.1) | async-done | bytes 262176 | tf_op jit(solution)/shard_map/all_to_all | solution.py:150
  113.4 0.2 fusion.14
  113.6 2.5 %fusion.10 = bf16[1,16,16,128]{3,1,2,0:T(8,128)(2,1)S(1)} fusion(f32[16,16,512]{2,0,1:T(8,128)S(1)} %fusion.26, bf16[16,512,128]{2,1,0:T(8,128)(2,1)} %param.18, f32[16,16,128]{2,1,0:T(8,128)S(1)} %fusion.14, f32[16,16]{0,1:T(8,128)S(1)} %get-tuple-element.5, f32[16,16]{0,1:T(8,128)S(1)} %get-tuple-element.7, f32[16,16]{0,1:T(8,128)S(1)} %get-tuple-element.6), kind=kOutput, calls=%fused_computation.21 | convolution fusion | flops 201490432 | bytes 2821120 | tf_op jit(solution)/shard_map/snhc,hcv->snhv/dot_general | solution.py:100
  116.2 0.2 stack.3
  116.4 50.4 %all_to_all.45 = bf16[32,1,1,16,2048]{4,3,2,1,0:T(8,128)(2,1)S(1)} all-to-all(bf16[32,1,1,16,2048]{4,3,2,1,0:T(8,128)(2,1)S(1)} %stack.3), channel_id=1, replica_groups=mesh['ctx'=4,'tp'=8,'dec'=8] {'ctx','dec'}, dimensions={0} | all-to-all | bytes 4194304 | tf_op jit(solution)/shard_map/all_to_all | solution.py:172
  166.8 0.8 fusion.4
  167.7 16.3 %all_to_all.46 = bf16[8,8,8,224]{3,2,1,0:T(8,128)(2,1)S(1)} all-to-all(bf16[8,8,8,224]{3,2,1,0:T(8,128)(2,1)S(1)} %copy.139), channel_id=1, replica_groups=mesh['ctx'=4,'tp'=8,'dec'=8] {'tp'}, dimensions={0} | all-to-all | bytes 458752 | tf_op jit(solution)/shard_map/all_to_all | solution.py:49
  184.0 0.7 reduce_sum.55
  (40 shorter events, 0.5 us)
Async XLA Ops:
  0.0 11.2 %copy-start = (bf16[16,128,512]{2,1,0:T(8,128)(2,1)S(1)}, bf16[16,128,512]{2,1,0:T(8,128)(2,1)}, u32[]{:S(2)}) copy-start(bf16[16,128,512]{2,1,0:T(8,128)(2,1)} %param.17) | copy-start | bytes 6291460
  3.4 6.3 %copy-start.3 = (bf16[1,64,16,64]{3,2,1,0:T(8,128)(2,1)S(1)}, bf16[1,64,16,64]{3,2,1,0:T(8,128)(2,1)}, u32[]{:S(2)}) copy-start(bf16[1,64,16,64]{3,2,1,0:T(8,128)(2,1)} %param.15) | copy-start | bytes 393220
  3.4 6.4 %copy-start.9 = (s32[1,64]{1,0:T(1,128)S(1)}, s32[1,64]{1,0:T(1,128)}, u32[]{:S(2)}) copy-start(s32[1,64]{1,0:T(1,128)} %param.13) | copy-start | bytes 772
  3.4 35.3 %all-to-all-start = ((bf16[8,1,256,577]{2,3,1,0:T(8,128)(2,1)}), bf16[8,1,256,577]{2,3,1,0:T(8,128)(2,1)}, u32[]{:S(2)}, u32[]{:S(2)}) async-start(bf16[8,1,256,577]{2,3,1,0:T(8,128)(2,1)} %broadcast_in_dim.58), calls=%async_computation | async-start | bytes 4784128 | tf_op jit(solution)/shard_map/all_to_all | solution.py:16
  11.2 1.5 copy-start.8
  11.2 1.5 copy-start.4
  13.6 0.7 copy-start.7
  62.1 5.5 %copy-start.10 = (f32[8]{0:T(128)S(1)}, f32[8]{0:T(128)}, u32[]{:S(2)}) copy-start(f32[8]{0:T(128)} %bitcast_convert_fusion) | copy-start | bytes 100
  67.6 2.5 %copy-start.2 = (bf16[64,16,576]{2,0,1:T(8,128)(2,1)S(1)}, bf16[64,16,576]{2,0,1:T(8,128)(2,1)}, u32[]{:S(2)}) copy-start(bf16[64,16,576]{2,0,1:T(8,128)(2,1)} %fusion.2) | copy-start | bytes 3538948
  75.9 14.2 %all-to-all-start.2 = ((bf16[4,2,128]{2,1,0:T(2,128)(2,1)}), bf16[4,2,128]{2,1,0:T(2,128)(2,1)S(1)}, u32[]{:S(2)}, u32[]{:S(2)}) async-start(bf16[4,2,128]{2,1,0:T(2,128)(2,1)} %reshape.539), calls=%async_computation.2 | async-start | bytes 4096 | tf_op jit(solution)/shard_map/all_to_all | solution.py:150
  83.6 1.6 copy-start.1
  85.1 20.6 %copy-start.5 = (f32[16,16]{0,1:T(8,128)S(1)}, f32[16,16]{0,1:T(8,128)}, u32[]{:S(2)}) copy-start(f32[16,16]{0,1:T(8,128)} %copy.129) | copy-start | bytes 3076
  85.1 20.6 %copy-start.6 = (f32[16,16]{0,1:T(8,128)S(1)}, f32[16,16]{0,1:T(8,128)}, u32[]{:S(2)}) copy-start(f32[16,16]{0,1:T(8,128)} %copy.136) | copy-start | bytes 3076
  90.1 11.9 %all-to-all-start.3 = ((bf16[4,2,128]{2,1,0:T(2,128)(2,1)}), bf16[4,2,128]{2,1,0:T(2,128)(2,1)S(1)}, u32[]{:S(2)}, u32[]{:S(2)}) async-start(bf16[4,2,128]{2,1,0:T(2,128)(2,1)} %reshape.541), calls=%async_computation.3 | async-start | bytes 4096 | tf_op jit(solution)/shard_map/all_to_all | solution.py:150
  102.0 11.4 %all-to-all-start.1 = ((bf16[1,1,64,16,128]{4,3,1,0,2:T(8,128)(2,1)}), bf16[1,1,64,16,128]{4,3,1,0,2:T(8,128)(2,1)S(1)}, u32[]{:S(2)}, u32[]{:S(2)}) async-start(bf16[1,1,64,16,128]{4,3,1,0,2:T(8,128)(2,1)} %copy.122), calls=%async_computation.1 | async-start | bytes 524288 | tf_op jit(solution)/shard_map/all_to_all | solution.py:150
  116.4 50.4 %copy-start.11 = (bf16[2048,224]{0,1:T(8,128)(2,1)S(1)}, bf16[2048,224]{0,1:T(8,128)(2,1)}, u32[]{:S(2)}) copy-start(bf16[2048,224]{0,1:T(8,128)(2,1)} %param.19) | copy-start | bytes 2752516
